TPU v7x, 32 devices: a whole 2x2x4 slice. The times are simulated.
32 devices in a mesh: dp: 8 (over z, x), tensor: 4 (over y, core).
Axes of the slice: x: 2, y: 2, z: 4, core: 2. Of those that a mesh axis runs over, the one named last changes fastest.
Arguments:
- activations: bfloat16 [4096, 16384], P('dp', 'tensor'), may hold values from -40 to 40, as said below
- token_ids: int32 [4096], P('dp'), may hold values from 0 to 128004, as said below
- weight: bfloat16 [16384, 16384], P('dp', 'tensor'), may hold values from -6 to 6
- inv_chol: float32 [128, 128, 1024], P('tensor', 'dp'), may hold values from -1 to 2, as said below
- bit_widths: int32 [128], P('tensor'), may hold values from 2 to 8, as said below
Outputs:
- quantized: bfloat16 [16384, 16384], P('dp', 'tensor')
- gram_blocks: float32 [128, 128, 128], P('tensor', 'dp')
- block_errors: float32 [128, 4], replicated
Inputs may be any that keep to these rules, and one draw needn't show every extreme that they name: `token_ids`: id 128004 marks padding. In the d-th aligned block of 512 tokens (d = 0 .. 7), exactly 170 + d*342//7 tokens are not padding, at positions drawn from the seed; the last block has no padding. `bit_widths`: each entry is 2, 3, 4 or 8. `inv_chol`: row i of block b, with j = b mod (8), holds a positive entry at column j*128+i, arbitrary entries at columns from (j+1)*128 on, and zeros elsewhere. `activations`: finite values.
All inputs are finite; a program needn't handle non-finite values.
Results may differ from a plain program's by a relative error of at most 0.001.
Values sent between devices are 32-bit elements; how exact they have to be, the bound alone decides.
A program may use at most 192 MiB of HBM per device.

v0:
```python
import jax
import jax.numpy as jnp
from jax import lax
from jax.sharding import PartitionSpec as P

OUT = 16384
BLK = 128
PANEL = 1024


pad_token = 128004


def level_count(widths):
    return jnp.where(
        widths == 2, 2.0, jnp.where(widths == 3, 4.0, jnp.where(widths == 4, 8.0, 128.0))
    ).astype(jnp.float32)


def soft_quantize(values, levels):
    largest = jnp.max(jnp.abs(values), axis=-1, keepdims=True)
    step_size = (largest + 1e-06) / (levels - 0.5)
    scaled = values / step_size
    smooth = scaled - jnp.sin(2.0 * jnp.pi * scaled) / (2.0 * jnp.pi)
    return step_size * jnp.clip(smooth, -levels, levels - 1.0)


def per_device(activations, token_ids, weight, inv_chol, bit_widths):
    token_count, width = activations.shape
    row_count = weight.shape[0]
    blocks_here = width // BLK
    panels_here = width // PANEL
    per_panel = PANEL // BLK
    live = token_ids != pad_token
    live_local = jnp.sum(live.astype(jnp.float32))
    masked = activations * live.astype(activations.dtype)[:, None]
    partial_gram = jnp.einsum(
        "tbi,tbj->bij",
        masked.reshape(token_count, blocks_here, BLK),
        activations.reshape(token_count, blocks_here, BLK),
        preferred_element_type=jnp.float32,
    )
    gram_sum, count = lax.psum((partial_gram, live_local), "dp")
    gram = gram_sum / count
    owned_rows = BLK // lax.axis_size("dp")
    gram_out = lax.dynamic_slice_in_dim(gram, lax.axis_index("dp") * owned_rows, owned_rows, 1)
    initial = weight.astype(jnp.float32).reshape(row_count, blocks_here, BLK)
    error_terms = []
    for levels in (2.0, 4.0, 8.0, 128.0):
        delta = initial - soft_quantize(initial, levels)
        weighted = jnp.einsum("rbi,bij->rbj", delta, gram, precision=lax.Precision.HIGHEST)
        error_terms.append(jnp.sum(weighted * delta, axis=(0, 2)) * (levels * levels / (OUT * BLK)))
    partial_errors = jnp.stack(error_terms, axis=1)
    summed_rows = lax.psum(partial_errors, "dp")
    block_errors = lax.all_gather(summed_rows, "tensor", axis=0, tiled=True)
    level_panels = level_count(bit_widths).reshape(panels_here, per_panel)
    factor_whole = lax.all_gather(inv_chol, "dp", axis=1, tiled=True).reshape(
        panels_here, per_panel, BLK, PANEL
    )
    current = weight.astype(jnp.float32).reshape(row_count, panels_here, PANEL)
    outputs = []
    for column_block in range(per_panel):
        first_column = column_block * BLK
        block_values = current[:, :, first_column : first_column + BLK]
        block_levels = level_panels[:, column_block][None, :, None]
        quantized_block = soft_quantize(block_values, block_levels)
        outputs.append(quantized_block.astype(jnp.bfloat16))
        if column_block + 1 < per_panel:
            factor_block = factor_whole[:, column_block, :, first_column:]
            diagonal = jnp.diagonal(factor_block[:, :, :BLK], axis1=1, axis2=2)
            scaled_error = (block_values - quantized_block) / diagonal[None, :, :]
            update = jnp.einsum(
                "rpi,pij->rpj",
                scaled_error,
                factor_block[:, :, BLK:],
                precision=lax.Precision.HIGHEST,
            )
            current = jnp.concatenate(
                [current[:, :, : first_column + BLK], current[:, :, first_column + BLK :] - update],
                axis=2,
            )
    quantized = jnp.concatenate(outputs, axis=2).reshape(row_count, width)
    return (quantized, gram_out, block_errors)


def solution(mesh):
    placed = (P("dp", "tensor"), P("dp"), P("dp", "tensor"), P("tensor", "dp", None), P("tensor"))
    return jax.shard_map(
        per_device,
        mesh=mesh,
        in_specs=placed,
        out_specs=(P("dp", "tensor"), P("tensor", "dp", None), P()),
        check_vma=False,
    )
```

profile of v0, /device:TPU:0, one launch (start us, length us, event | category | flops | bytes accessed | tf_op | source)
XLA Modules:
  0.0 1832.3 jit_solution(16052854289736793508)
XLA Ops:
  26.9 24.8 %psum.22 = f32[]{:T(128)} all-reduce(f32[]{:T(128)} %get-tuple-element.36), channel_id=1, replica_groups=mesh['dp'=8,'tensor'=4] {'dp'}, use_global_device_ids=true, to_apply=%region_10.11 | all-reduce | flops 1 | bytes 8 | tf_op jit(solution)/shard_map/psum | solution.py:43
  52.9 23.9 %copy.84 = f32[2048,4096]{0,1:T(8,128)} copy(bf16[2048,4096]{1,0:T(8,128)(2,1)} %param.7) | data formatting | bytes 50331648 | tf_op jit(solution)/shard_map/convert_element_type | solution.py:60
  92.8 16.7 convert_dynamic-update-slice_fusion.6
  109.5 21.0 %all-reduce.2.cloned.1.call-done = f32[32,128,128]{2,1,0:T(8,128)} async-done(((f32[32,128,128]{2,1,0:T(8,128)}), f32[32,128,128]{2,1,0:T(8,128)}) %all-reduce.2.cloned.1.call-update) | async-done | bytes 2097168 | tf_op jit(solution)/shard_map/psum | solution.py:43
  133.3 284.2 %fusion.3 = f32[32]{0:T(128)S(1)} fusion(f32[32,128,128]{2,1,0:T(8,128)S(1)} %broadcast_divide_fusion, f32[2048,32,128]{0,2,1:T(8,128)} %bitcast.85, f32[2048,32]{0,1:T(8,128)S(1)} %get-tuple-element.38), kind=kOutput, calls=%fused_computation.14 | convolution fusion | flops 13019119616 | bytes 35913856 | tf_op jit(solution)/shard_map/rbi,bij->rbj/dot_general | solution.py:51
  417.6 301.9 %fusion.2 = f32[32]{0:T(128)S(1)} fusion(f32[32,128,128]{2,1,0:T(8,128)S(1)} %broadcast_divide_fusion, f32[2048,32,128]{0,2,1:T(8,128)S(1)} %bitcast.89, f32[2048,32]{0,1:T(8,128)S(1)} %get-tuple-element.39), kind=kOutput, calls=%fused_computation.12 | convolution fusion | flops 13019119616 | bytes 35913856 | tf_op jit(solution)/shard_map/rbi,bij->rbj/dot_general | solution.py:51
  720.0 301.8 %fusion.1 = f32[32]{0:T(128)S(1)} fusion(f32[32,128,128]{2,1,0:T(8,128)S(1)} %broadcast_divide_fusion, f32[2048,32,128]{0,2,1:T(8,128)S(1)} %bitcast.90, f32[2048,32]{0,1:T(8,128)S(1)} %copy-done.14), kind=kOutput, calls=%fused_computation.10 | convolution fusion | flops 13019119616 | bytes 35913856 | tf_op jit(solution)/shard_map/rbi,bij->rbj/dot_general | solution.py:51
  1021.8 301.9 %fusion = f32[32]{0:T(128)S(1)} fusion(f32[32,128,128]{2,1,0:T(8,128)S(1)} %broadcast_divide_fusion, f32[2048,32,128]{0,2,1:T(8,128)S(1)} %bitcast.91, f32[2048,32]{0,1:T(8,128)S(1)} %copy-done.13), kind=kOutput, calls=%fused_computation.8 | convolution fusion | flops 13019119616 | bytes 35913856 | tf_op jit(solution)/shard_map/rbi,bij->rbj/dot_general | solution.py:51
  1323.8 20.0 %psum.23 = f32[32,4]{0,1:T(4,128)S(1)} all-reduce(f32[32,4]{0,1:T(4,128)S(1)} %pad_maximum_fusion), channel_id=1, replica_groups=mesh['dp'=8,'tensor'=4] {'dp'}, use_global_device_ids=true, to_apply=%region_16.17 | all-reduce | flops 128 | bytes 1024 | tf_op jit(solution)/shard_map/psum | solution.py:54
  1456.5 43.7 %slice_subtract_fusion = f32[2048,4,896]{0,2,1:T(8,128)} fusion(f32[2048,4,1024]{0,2,1:T(8,128)} %bitcast.86, f32[4,128]{1,0:T(4,128)S(1)} %copy.87, f32[4,128,1024]{1,2,0:T(8,128)S(1)} %bitcast.101, f32[4]{0:T(128)S(1)} %copy-done.41, f32[4]{0:T(128)S(1)} %copy-done.43, f32[2048,4]{0,1:T(4,128)S(1)} %copy-done.16), kind=kOutput, calls=%fused_computation.20 | convolution fusion | flops 11291066368 | bytes 64785408 | tf_op jit(solution)/shard_map/rpi,pij->rpj/dot_general | solution.py:72
  1502.8 16.7 convert_dynamic-update-slice_fusion.5
  1519.5 38.2 %slice_subtract_fusion.1 = f32[2048,4,768]{0,2,1:T(8,128)S(1)} fusion(f32[2048,4,896]{0,2,1:T(8,128)} %slice_subtract_fusion, f32[4,128]{1,0:T(4,128)S(1)} %copy.91, f32[4,128,896]{1,2,0:T(8,128)S(1)} %bitcast.103, f32[4]{0:T(128)S(1)} %copy-done.38, f32[4]{0:T(128)S(1)} %copy-done.39, f32[2048,4]{0,1:T(4,128)S(1)} %add_divide_fusion.6), kind=kOutput, calls=%fused_computation.21 | convolution fusion | flops 9679405056 | bytes 56134656 | tf_op jit(solution)/shard_map/rpi,pij->rpj/dot_general | solution.py:72
  1566.7 15.3 convert_dynamic-update-slice_fusion.4
  1582.0 36.0 %slice_subtract_fusion.2 = f32[2048,4,640]{0,2,1:T(8,128)S(1)} fusion(f32[2048,4,768]{0,2,1:T(8,128)} %copy-done.2, f32[4,128]{1,0:T(4,128)S(1)} %copy.95, f32[4,128,768]{1,2,0:T(8,128)S(1)} %bitcast.105, f32[4]{0:T(128)S(1)} %copy-done.36, f32[4]{0:T(128)S(1)} %copy-done.37, f32[2048,4]{0,1:T(4,128)S(1)} %add_divide_fusion.5), kind=kOutput, calls=%fused_computation.22 | convolution fusion | flops 8067743744 | bytes 47483904 | tf_op jit(solution)/shard_map/rpi,pij->rpj/dot_general | solution.py:72
  1625.4 15.3 convert_dynamic-update-slice_fusion.3
  1640.7 32.1 %slice_subtract_fusion.3 = f32[2048,4,512]{0,2,1:T(8,128)S(1)} fusion(f32[2048,4,640]{0,2,1:T(8,128)} %copy-done.1, f32[4,128]{1,0:T(4,128)S(1)} %copy.99, f32[4,128,640]{1,2,0:T(8,128)S(1)} %bitcast.107, f32[4]{0:T(128)S(1)} %copy-done.34, f32[4]{0:T(128)S(1)} %copy-done.35, f32[2048,4]{0,1:T(4,128)S(1)} %add_divide_fusion.4), kind=kOutput, calls=%fused_computation.23 | convolution fusion | flops 6456082432 | bytes 38833152 | tf_op jit(solution)/shard_map/rpi,pij->rpj/dot_general | solution.py:72
  1673.4 15.5 convert_dynamic-update-slice_fusion.2
  1688.9 25.2 %slice_subtract_fusion.4 = f32[2048,4,384]{0,2,1:T(8,128)S(1)} fusion(f32[2048,4,512]{0,2,1:T(8,128)S(1)} %slice_subtract_fusion.3, f32[4,128]{1,0:T(4,128)S(1)} %copy.103, f32[4,128,512]{1,2,0:T(8,128)S(1)} %bitcast.109, f32[4]{0:T(128)S(1)} %copy-done.32, f32[4]{0:T(128)S(1)} %copy-done.33, f32[2048,4]{0,1:T(4,128)S(1)} %add_divide_fusion.3), kind=kOutput, calls=%fused_computation.44 | convolution fusion | flops 4844421120 | bytes 30182400 | tf_op jit(solution)/shard_map/rpi,pij->rpj/dot_general | solution.py:72
  1714.9 15.3 convert_dynamic-update-slice_fusion.1
  1730.2 22.4 %slice_subtract_fusion.5 = f32[2048,4,256]{0,2,1:T(8,128)S(1)} fusion(f32[2048,4,384]{0,2,1:T(8,128)S(1)} %slice_subtract_fusion.4, f32[4,128]{1,0:T(4,128)S(1)} %copy.107, f32[4,128,384]{1,2,0:T(8,128)S(1)} %bitcast.111, f32[4]{0:T(128)S(1)} %copy-done.30, f32[4]{0:T(128)S(1)} %copy-done.31, f32[2048,4]{0,1:T(4,128)S(1)} %add_divide_fusion.2), kind=kOutput, calls=%fused_computation.45 | convolution fusion | flops 3232759808 | bytes 21531648 | tf_op jit(solution)/shard_map/rpi,pij->rpj/dot_general | solution.py:72
  1753.4 15.3 convert_dynamic-update-slice_fusion
  1768.7 19.7 %abs_reduce_fusion.1 = (f32[2048,4]{0,1:T(4,128)S(1)}, f32[2048,4,128]{0,2,1:T(8,128)S(1)}) fusion(f32[4,128,256]{1,2,0:T(8,128)S(1)} %bitcast.113, f32[2048,4,256]{0,2,1:T(8,128)S(1)} %slice_subtract_fusion.5, f32[4,128]{1,0:T(4,128)S(1)} %copy.111, f32[4]{0:T(128)S(1)} %copy-done.28, f32[4]{0:T(128)S(1)} %copy-done.29, f32[2048,4]{0,1:T(4,128)S(1)} %add_divide_fusion.1), kind=kOutput, calls=%fused_computation.51 | convolution fusion | flops 1623187456 | bytes 12913664 | tf_op jit(solution)/shard_map/rpi,pij->rpj/dot_general | solution.py:72
  1788.5 15.3 fusion.51
  1803.8 21.2 %copy.125 = bf16[2048,4096]{1,0:T(8,128)(2,1)} copy(bf16[2048,4096]{0,1:T(8,128)(2,1)} %bitcast.24) | data formatting | bytes 33554432
  (188 shorter events, 173.8 us)
Async XLA Ops:
  7.2 123.3 %all-reduce.2.cloned.1.call-start = ((), (), s32[]{:S(2)}) async-start(), calls=%async_computation.1 | async-start | bytes 4194304 | tf_op jit(solution)/shard_map/psum | solution.py:43
  25.6 1325.1 %all-gather.3.cloned.1.call-start = ((), (), s32[]{:S(2)}) async-start(), calls=%async_computation | async-start | bytes 18874368 | tf_op jit(solution)/shard_map/all_gather | solution.py:57
  52.9 39.3 %copy-start.40 = (f32[4]{0:T(128)}, f32[4]{0:T(128)S(1)}, u32[]{:S(2)}) copy-start(f32[4]{0:T(128)S(1)} %get-tuple-element.58) | copy-start | bytes 52
  52.9 39.3 %copy-start.42 = (f32[4]{0:T(128)}, f32[4]{0:T(128)S(1)}, u32[]{:S(2)}) copy-start(f32[4]{0:T(128)S(1)} %get-tuple-element.59) | copy-start | bytes 52
  130.5 287.0 %slice-start = ((s8[33554432]{0:T(1024)(128)(4,1)}), s8[4194304]{0:T(1024)(128)(4,1)S(1)}, s32[]{:S(2)}) async-start(s8[33554432]{0:T(1024)(128)(4,1)} %bitcast.87), calls=%async_computation.2 | async-start | bytes 8388608
  133.3 284.2 %slice-start.1 = ((s8[33554432]{0:T(1024)(128)(4,1)}), s8[4194304]{0:T(1024)(128)(4,1)S(1)}, s32[]{:S(2)}) async-start(s8[33554432]{0:T(1024)(128)(4,1)} %bitcast.87), calls=%async_computation.3 | async-start | bytes 8388608
  133.3 284.2 %slice-start.2 = ((s8[33554432]{0:T(1024)(128)(4,1)}), s8[4194304]{0:T(1024)(128)(4,1)S(1)}, s32[]{:S(2)}) async-start(s8[33554432]{0:T(1024)(128)(4,1)} %bitcast.87), calls=%async_computation.4 | async-start | bytes 8388608
  133.3 284.2 %slice-start.3 = ((s8[33554432]{0:T(1024)(128)(4,1)}), s8[4194304]{0:T(1024)(128)(4,1)S(1)}, s32[]{:S(2)}) async-start(s8[33554432]{0:T(1024)(128)(4,1)} %bitcast.87), calls=%async_computation.5 | async-start | bytes 8388608
  133.3 284.2 %slice-start.4 = ((s8[33554432]{0:T(1024)(128)(4,1)}), s8[4194304]{0:T(1024)(128)(4,1)S(1)}, s32[]{:S(2)}) async-start(s8[33554432]{0:T(1024)(128)(4,1)} %bitcast.87), calls=%async_computation.6 | async-start | bytes 8388608
  133.3 284.2 %slice-start.5 = ((s8[33554432]{0:T(1024)(128)(4,1)}), s8[4194304]{0:T(1024)(128)(4,1)S(1)}, s32[]{:S(2)}) async-start(s8[33554432]{0:T(1024)(128)(4,1)} %bitcast.87), calls=%async_computation.7 | async-start | bytes 8388608
  133.3 284.2 %slice-start.6 = ((s8[33554432]{0:T(1024)(128)(4,1)}), s8[4194304]{0:T(1024)(128)(4,1)S(1)}, s32[]{:S(2)}) async-start(s8[33554432]{0:T(1024)(128)(4,1)} %bitcast.87), calls=%async_computation.8 | async-start | bytes 8388608
  133.3 284.2 %slice-start.7 = ((s8[33554432]{0:T(1024)(128)(4,1)}), s8[4194304]{0:T(1024)(128)(4,1)S(1)}, s32[]{:S(2)}) async-start(s8[33554432]{0:T(1024)(128)(4,1)} %bitcast.87), calls=%async_computation.9 | async-start | bytes 8388608
  417.6 302.4 %copy-start.14 = (f32[2048,32]{0,1:T(8,128)S(1)}, f32[2048,32]{0,1:T(8,128)}, u32[]{:S(2)}) copy-start(f32[2048,32]{0,1:T(8,128)} %get-tuple-element.40) | copy-start | bytes 786436
  720.0 301.8 %copy-start.13 = (f32[2048,32]{0,1:T(8,128)S(1)}, f32[2048,32]{0,1:T(8,128)}, u32[]{:S(2)}) copy-start(f32[2048,32]{0,1:T(8,128)} %get-tuple-element.41) | copy-start | bytes 786436
  1021.8 301.9 %copy-start.24 = (f32[32,1]{0,1:T(1,128)S(1)}, f32[32,1]{0,1:T(1,128)}, u32[]{:S(2)}) copy-start(f32[32,1]{0,1:T(1,128)} %get-tuple-element.65) | copy-start | bytes 388
  1021.8 301.9 %copy-start.25 = (f32[32,1]{0,1:T(1,128)S(1)}, f32[32,1]{0,1:T(1,128)}, u32[]{:S(2)}) copy-start(f32[32,1]{0,1:T(1,128)} %get-tuple-element.66) | copy-start | bytes 388
  1502.7 16.9 copy-start.4
  1558.2 23.8 %copy-start.5 = (f32[4,1,128,768]{2,3,0,1:T(8,128)S(1)}, f32[4,1,128,768]{2,3,0,1:T(8,128)}, u32[]{:S(2)}) copy-start(f32[4,1,128,768]{2,3,0,1:T(8,128)} %copy.144) | copy-start | bytes 4718596
  1618.4 22.3 %copy-start.6 = (f32[4,1,128,640]{2,3,0,1:T(8,128)S(1)}, f32[4,1,128,640]{2,3,0,1:T(8,128)}, u32[]{:S(2)}) copy-start(f32[4,1,128,640]{2,3,0,1:T(8,128)} %copy.145) | copy-start | bytes 3932164
  1673.1 15.8 copy-start.7
  1714.5 15.7 copy-start.8
  1768.7 19.7 %copy-start.17 = (f32[4]{0:T(128)S(1)}, f32[4]{0:T(128)}, u32[]{:S(2)}) copy-start(f32[4]{0:T(128)} %get-tuple-element.60) | copy-start | bytes 52
  1768.7 19.8 %copy-start.26 = (f32[4]{0:T(128)S(1)}, f32[4]{0:T(128)}, u32[]{:S(2)}) copy-start(f32[4]{0:T(128)} %get-tuple-element.44) | copy-start | bytes 52
  1768.7 19.8 %copy-start.27 = (f32[4]{0:T(128)S(1)}, f32[4]{0:T(128)}, u32[]{:S(2)}) copy-start(f32[4]{0:T(128)} %get-tuple-element.45) | copy-start | bytes 52
  (31 other events, 150.6 us)
Sparse Core Ops, SparseCore 0:
  25.7 104.7 all-reduce.1
  132.7 227.2 all-gather.2
where the time goes:
time: 1840 us; the launch traced here: 1830 us
  matrix products  1410 us (77%)
  local copies, waits for them, and re-layouts  176 us (10%)
  other arithmetic  156 us (8%)
  blocking collectives  50.4 us (3%)
  waiting for transfers between devices  21.7 us (1%)
    dot_general x4, matrix products, per_device(): jnp.einsum('rbi,bij->rbj', delta, gram, precision=lax.Precision.HIGHEST)  1190 us
    dot_general x7, matrix products, per_device(): jnp.einsum('rpi,pij->rpj', scaled_error, factor_block[:, :, BLK:], precis...  217 us
    unnamed x8, other arithmetic  110 us
    slice x14, local copies, waits for them, and re-layouts, per_device(): diagonal = jnp.diagonal(factor_block[:, :, :BLK], axis1=1, axis2=2)  60.9 us
    unnamed x115, local copies, waits for them, and re-layouts  55 us
  transfers between devices with their start and end apart: 2, of which 1 were waited for; matrix products, arithmetic and copies ran while one was open for 68% of the time, Pallas kernels for 0%

commit v1 on v0

v1 whole, which is shorter than its diff:
```python
import functools
import math

import jax
import jax.numpy as jnp
from jax import lax
from jax.experimental import pallas as pl
from jax.experimental.pallas import tpu as pltpu
from jax.sharding import PartitionSpec as P

BLK = 128
PANEL = 1024
PER = PANEL // BLK
PAIR = 2 * BLK

pad_token = 128004

SINE = (
    0.9999996039174559,
    -6.579691569594437,
    12.986435989563077,
    -12.18810142777418,
    6.5580417797975565,
    -1.9530312812214594,
)
MIB = 1024 * 1024


def sine_turn(r):
    square = r * r
    total = SINE[-1] * square + SINE[-2]
    for factor in SINE[-3::-1]:
        total = total * square + factor
    return r * total


def row_dot(a, b):
    return lax.dot_general(a, b, (((0,), (0,)), ((), ())), preferred_element_type=jnp.float32)


def dot(a, b):
    return jnp.dot(a, b, preferred_element_type=jnp.float32)


def gram_kernel(steps, x_ref, id_ref, out_ref):
    step = pl.program_id(0)
    live = jnp.where(id_ref[...] != pad_token, 1.0, 0.0).astype(jnp.float32)

    @pl.when(step < steps)
    def _():
        x = x_ref[...]
        masked = (x.astype(jnp.float32) * live).astype(x.dtype)
        whole = row_dot(masked, x)
        out_ref[0] = whole[:BLK, :BLK]
        out_ref[1] = whole[BLK:, BLK:]

    @pl.when(step == steps)
    def _():
        count = jnp.sum(live, axis=0, keepdims=True)
        out_ref[...] = jnp.broadcast_to(count[None], out_ref.shape)


def gram_sums(activations, token_ids):
    tokens, width = activations.shape
    steps = width // PAIR
    return pl.pallas_call(
        functools.partial(gram_kernel, steps),
        grid=(steps + 1,),
        in_specs=[
            pl.BlockSpec((tokens, PAIR), lambda i: (0, jnp.minimum(i, steps - 1))),
            pl.BlockSpec((tokens, 1), lambda i: (0, 0)),
        ],
        out_specs=pl.BlockSpec((2, BLK, BLK), lambda i: (i, 0, 0)),
        out_shape=jax.ShapeDtypeStruct((2 * steps + 2, BLK, BLK), jnp.float32),
        compiler_params=pltpu.CompilerParams(vmem_limit_bytes=32 * MIB),
        cost_estimate=pl.CostEstimate(
            flops=2 * tokens * width * PAIR, bytes_accessed=2 * tokens * width, transcendentals=0
        ),
        name="gram_sums",
    )(activations, token_ids.reshape(tokens, 1))


PI = math.pi


def clipped(smooth, levels):
    half = levels - 0.5
    return jnp.clip(smooth, -levels / half, (levels - 1.0) / half)


def block_deltas(piece):
    w = piece.astype(jnp.float32)
    largest = jnp.max(jnp.abs(w), axis=-1, keepdims=True) + 1e-6
    v = w * (1.0 / largest)
    sine = sine_turn(0.5 * v) * (2.0 * PI)
    square = sine * sine
    third = sine * ((-4.0 / (3.0 * PI)) * square + (3.0 / (3.0 * PI)))
    c = 1.0 / (7.0 * PI)
    seventh = sine * (((-64.0 * c * square + 112.0 * c) * square - 56.0 * c) * square + 7.0 * c)
    x2 = third * third
    k = (3.0 * PI) ** 2
    fifteenth = third * ((3.2 * k * k * x2 - 4.0 * k) * x2 + 1.0)
    turns = 127.5 * v
    last = sine_turn(turns - jnp.round(turns)) * (1.0 / 127.5)
    out = []
    for levels, term in ((2.0, third), (4.0, seventh), (8.0, fifteenth), (128.0, last)):
        out.append(((v - clipped(v - term, levels)) * largest).astype(jnp.bfloat16))
    return out


def error_kernel(rows, sub, w_ref, out_ref):
    @pl.when(pl.program_id(1) == 0)
    def _():
        out_ref[...] = jnp.zeros_like(out_ref)

    @pl.loop(0, w_ref.shape[1] // BLK)
    def _(block):
        columns = pl.ds(pl.multiple_of(block * BLK, BLK), BLK)
        first = second = None
        for start in range(0, rows, sub):
            pieces = [
                block_deltas(w_ref[pl.ds(at, 32), columns]) for at in range(start, start + sub, 32)
            ]
            e = [jnp.concatenate([p[i] for p in pieces], axis=0) for i in range(4)]
            low = jnp.concatenate(e[:2], axis=1)
            high = jnp.concatenate(e[2:], axis=1)
            a, b = row_dot(low, low), row_dot(high, high)
            first = a if first is None else first + a
            second = b if second is None else second + b
        out_ref[block, 0] += first[:BLK, :BLK]
        out_ref[block, 1] += first[BLK:, BLK:]
        out_ref[block, 2] += second[:BLK, :BLK]
        out_ref[block, 3] += second[BLK:, BLK:]


def error_products(weight, first_panel, panels):
    row_count, width = weight.shape[0], panels * PANEL
    rows = min(512, row_count)
    sub = 256
    return pl.pallas_call(
        functools.partial(error_kernel, rows, sub),
        grid=(width // PANEL, row_count // rows),
        in_specs=[pl.BlockSpec((rows, PANEL), lambda p, r: (r, p + first_panel))],
        out_specs=pl.BlockSpec((PER, 4, BLK, BLK), lambda p, r: (p, 0, 0, 0)),
        out_shape=jax.ShapeDtypeStruct((width // BLK, 4, BLK, BLK), jnp.float32),
        compiler_params=pltpu.CompilerParams(vmem_limit_bytes=32 * MIB),
        cost_estimate=pl.CostEstimate(
            flops=85 * row_count * width * PAIR,
            bytes_accessed=2 * row_count * width,
            transcendentals=0,
        ),
        name="error_products",
    )(weight)


def split(value):
    high = value.astype(jnp.bfloat16)
    return high, (value - high.astype(jnp.float32)).astype(jnp.bfloat16)


def quantize_block(current, levels):
    out, high, low = [], [], []
    for at in range(0, current.shape[0], 64):
        c = current[at : at + 64]
        largest = jnp.max(jnp.abs(c), axis=-1, keepdims=True) + 1e-6
        step = largest / (levels - 0.5)
        u = c * ((levels - 0.5) / largest)
        smooth = u - sine_turn(u - jnp.round(u))
        q = step * jnp.clip(smooth, -levels, levels - 1.0)
        out.append(q.astype(jnp.bfloat16))
        h, l = split(c - q)
        high.append(h)
        low.append(l)
    return tuple(jnp.concatenate(x, axis=0) for x in (out, high, low))


def panel_kernel(rows, streams, width_ref, w_ref, u_ref, out_ref, uh_ref, ul_ref, eh_ref, el_ref):
    panel = pl.program_id(0)

    @pl.when(pl.program_id(1) == 0)
    def _():
        for i in range(PER - 1):
            slot, first = (0, 0) if i == 0 else ((i, 0) if i < 4 else (7 - i, i * BLK))
            span = (PER - 1 - i) * BLK
            high, low = split(u_ref[0, slot, :, first : first + span])
            uh_ref[i * BLK : (i + 1) * BLK, (i + 1) * BLK :] = high
            ul_ref[i * BLK : (i + 1) * BLK, (i + 1) * BLK :] = low

    levels = []
    for j in range(PER):
        w = width_ref[panel * PER + j]
        levels.append(
            jnp.where(w == 2, 2.0, jnp.where(w == 3, 4.0, jnp.where(w == 4, 8.0, 128.0)))
        )
    part = rows // streams
    spans = [slice(s * part, (s + 1) * part) for s in range(streams)]
    for pair in range(PER // 2):
        left = slice(pair * PAIR, pair * PAIR + BLK)
        right = slice(pair * PAIR + BLK, (pair + 1) * PAIR)
        both = slice(pair * PAIR, (pair + 1) * PAIR)
        done = slice(0, pair * PAIR)
        current = []
        for span in spans:
            c = w_ref[span, both].astype(jnp.float32)
            if pair > 0:
                c = c - (
                    dot(eh_ref[span, done], uh_ref[done, both])
                    + dot(el_ref[span, done], uh_ref[done, both])
                    + dot(eh_ref[span, done], ul_ref[done, both])
                )
            current.append(c)
        halves = []
        for span, c in zip(spans, current):
            out, high, low = quantize_block(c[:, :BLK], levels[2 * pair])
            out_ref[span, left] = out
            halves.append((high, low))
        for span, c, (high, low) in zip(spans, current, halves):
            uh, ul = uh_ref[left, right], ul_ref[left, right]
            update = dot(
                jnp.concatenate([high, low], axis=1), jnp.concatenate([uh, uh], axis=0)
            ) + dot(high, ul)
            out, high2, low2 = quantize_block(c[:, BLK:] - update, levels[2 * pair + 1])
            out_ref[span, right] = out
            if pair + 1 < PER // 2:
                eh_ref[span, left] = high
                el_ref[span, left] = low
                eh_ref[span, right] = high2
                el_ref[span, right] = low2


def quantize_panels(weight, factor, bit_widths):
    row_count, width = weight.shape
    rows = min(512, row_count)
    kept = PANEL - PAIR
    return pl.pallas_call(
        functools.partial(panel_kernel, rows, 2),
        grid_spec=pltpu.PrefetchScalarGridSpec(
            num_scalar_prefetch=1,
            grid=(width // PANEL, row_count // rows),
            in_specs=[
                pl.BlockSpec((rows, PANEL), lambda p, r, s: (r, p)),
                pl.BlockSpec((1, PER // 2, BLK, PANEL - BLK), lambda p, r, s: (p, 0, 0, 0)),
            ],
            out_specs=pl.BlockSpec((rows, PANEL), lambda p, r, s: (r, p)),
            scratch_shapes=[
                pltpu.VMEM((PANEL, PANEL), jnp.bfloat16),
                pltpu.VMEM((PANEL, PANEL), jnp.bfloat16),
                pltpu.VMEM((rows, kept), jnp.bfloat16),
                pltpu.VMEM((rows, kept), jnp.bfloat16),
            ],
        ),
        out_shape=jax.ShapeDtypeStruct((row_count, width), jnp.bfloat16),
        compiler_params=pltpu.CompilerParams(vmem_limit_bytes=40 * MIB),
        cost_estimate=pl.CostEstimate(
            flops=40 * row_count * width * PAIR,
            bytes_accessed=4 * row_count * width,
            transcendentals=0,
        ),
        name="quantize_panels",
    )(bit_widths, weight, factor)


def scaled_rows(inv_chol):
    blocks, owned, width = inv_chol.shape
    panels = blocks // PER
    rows = inv_chol.reshape(panels, PER, owned, width)
    row = lax.broadcasted_iota(jnp.int32, (owned, BLK), 0) + lax.axis_index("dp") * owned
    mine = (lax.broadcasted_iota(jnp.int32, (owned, BLK), 1) == row)[None]
    parts = []
    for i in range(PER - 1):
        at = slice(i * BLK, (i + 1) * BLK)
        diagonal = jnp.sum(jnp.where(mine, rows[:, i, :, at], 0.0), axis=-1, keepdims=True)
        parts.append(rows[:, i, :, (i + 1) * BLK :] / diagonal)
    packed = [parts[0]] + [
        jnp.concatenate([parts[i], parts[PER - 1 - i]], axis=-1) for i in range(1, PER // 2)
    ]
    return jnp.stack(packed, axis=1)


def per_device(activations, token_ids, weight, inv_chol, bit_widths):
    blocks_here = weight.shape[1] // BLK
    out_rows = weight.shape[0] * lax.axis_size("dp")
    factor = lax.all_gather(scaled_rows(inv_chol), "dp", axis=2, tiled=True)
    partial = gram_sums(activations, token_ids)
    panels = weight.shape[1] // PANEL
    early = max(1, 3 * panels // 4)
    products = [error_products(weight, 0, early)]
    factor, partial, products[0], later_weight = lax.optimization_barrier(
        (factor, partial, products[0], weight)
    )
    gram_sum = lax.psum(partial, "dp")
    if early < panels:
        products.append(error_products(later_weight, early, panels - early))
    quantized = quantize_panels(later_weight, factor, bit_widths)
    gram_sum, quantized, *products = lax.optimization_barrier((gram_sum, quantized, *products))
    gram = gram_sum[:blocks_here] / gram_sum[blocks_here, 0, 0]
    owned = BLK // lax.axis_size("dp")
    gram_out = lax.dynamic_slice_in_dim(gram, lax.axis_index("dp") * owned, owned, 1)
    levels = jnp.array([2.0, 4.0, 8.0, 128.0], jnp.float32)
    sums, at = [], 0
    for part in products:
        sums.append(jnp.sum(part * gram[at : at + part.shape[0], None], axis=(2, 3)))
        at += part.shape[0]
    errors = jnp.concatenate(sums, axis=0) * (levels * levels / (out_rows * BLK))
    everywhere = jnp.zeros((blocks_here * lax.axis_size("tensor"), 4), jnp.float32)
    everywhere = lax.dynamic_update_slice(
        everywhere, errors, (lax.axis_index("tensor") * blocks_here, 0)
    )
    block_errors = lax.psum(everywhere, ("dp", "tensor"))
    return (quantized, gram_out, block_errors)


def solution(mesh):
    placed = (P("dp", "tensor"), P("dp"), P("dp", "tensor"), P("tensor", "dp", None), P("tensor"))
    return jax.shard_map(
        per_device,
        mesh=mesh,
        in_specs=placed,
        out_specs=(P("dp", "tensor"), P("tensor", "dp", None), P()),
        check_vma=False,
    )
```

time: 1840 us -> 303 us (0.16)
  matrix products: 1410 us -> 0 us
  Pallas kernels: 0 us -> 213 us
  local copies, waits for them, and re-layouts: 176 us -> 19.5 us
  other arithmetic: 156 us -> 12.6 us
  waiting for transfers between devices: 21.7 us -> 2.94 us
    dot_general x12 -> x0, matrix products: 1410 us -> none  [the longest x4 1190 us: per_device(): jnp.einsum('rbi,bij->rbj', delta, gram, precision=lax.Precision.HIGHEST)]
    pallas_call x0 -> x4, Pallas kernels: none -> 213 us  [the longest x2 130 us: error_products(): pl.pallas_call(functools.partial(error_kernel, rows, sub), grid=(width //...]
    unnamed x8 -> x0, other arithmetic: 110 us -> none
    slice x21 -> x4, local copies, waits for them, and re-layouts: 75.9 us -> 1.63 us  [the longest x1 1.19 us: per_device(): gram = gram_sum[:blocks_here] / gram_sum[blocks_here, 0, 0]]
    unnamed x115 -> x18, local copies, waits for them, and re-layouts: 55 us -> 15.8 us
    convert_element_type x1 -> x0, local copies, waits for them, and re-layouts: 23.9 us -> none  [per_device(): current = weight.astype(jnp.float32).reshape(row_count, panels_here, PANEL)]
    psum x1, waiting for transfers between devices: 21 us -> 0.02 us  [per_device(): gram_sum = lax.psum(partial, 'dp')]
    reduce_max x8 -> x0, other arithmetic: 18.6 us -> none  [soft_quantize(): largest = jnp.max(jnp.abs(values), axis=-1, keepdims=True)]
  transfers between devices with their start and end apart: 2 -> 2, of which waited for: 1 -> 1; matrix products, arithmetic and copies ran while one was open for 68% -> 0% of each run, Pallas kernels for 0% -> 71%
where the time goes in v1:
time: 303 us; the launch traced here: 302 us
  Pallas kernels  213 us (70%)
  blocking collectives  39.4 us (13%)
  local copies, waits for them, and re-layouts  19.5 us (6%)
  between operations  14.2 us (5%)
  other arithmetic  12.6 us (4%)
    pallas_call x2, Pallas kernels, error_products(): pl.pallas_call(functools.partial(error_kernel, rows, sub), grid=(width //...  130 us
    pallas_call x1, Pallas kernels, quantize_panels(): pl.pallas_call(functools.partial(panel_kernel, rows, 2), grid_spec=pltpu....  73.9 us
    psum x1, blocking collectives, per_device(): block_errors = lax.psum(everywhere, ('dp', 'tensor'))  39.4 us
    unnamed x18, local copies, waits for them, and re-layouts  15.8 us
    pallas_call x1, Pallas kernels, gram_sums(): pl.pallas_call(functools.partial(gram_kernel, steps), grid=(steps + 1,),...  9.44 us
    div x7, other arithmetic, scaled_rows(): parts.append(rows[:, i, :, (i + 1) * BLK:] / diagonal)  6.86 us
  transfers between devices with their start and end apart: 2, of which 1 were waited for; matrix products, arithmetic and copies ran while one was open for 0% of the time, Pallas kernels for 71%

profile of v1, /device:TPU:0, one launch (start us, length us, event | category | flops | bytes accessed | tf_op | source)
XLA Modules:
  0.0 301.8 jit_solution(6831781231211135572)
XLA Ops:
  7.3 1.0 fusion.19
  8.3 0.9 fusion.15
  9.2 1.0 fusion
  10.2 1.0 fusion.1
  11.2 0.9 fusion.4
  12.1 1.0 fusion.2
  13.1 1.0 fusion.3
  14.1 1.0 slice_divide_fusion.1
  15.3 1.0 pad_maximum_fusion
  16.5 2.2 copy-done.2
  18.7 9.4 %gram_sums.1 = f32[34,128,128]{2,1,0:T(8,128)} custom-call(bf16[512,4096]{1,0:T(8,128)(2,1)S(1)} %copy-done.2, s32[512,1]{1,0:T(8,128)S(1)} %copy.51.id_ref), custom_call_target="tpu_custom_call" | custom-call | flops 1073741824 | bytes 4194304 | tf_op jit(solution)/shard_map/gram_sums/pallas_call | solution.py:66
  28.1 97.4 %error_products.2 = f32[24,4,128,128]{3,2,1,0:T(8,128)S(1)} custom-call(bf16[2048,4096]{1,0:T(8,128)(2,1)} %w_ref.3), custom_call_target="tpu_custom_call" | custom-call | flops 136902082560 | bytes 12582912 | tf_op jit(solution)/shard_map/error_products/pallas_call | solution.py:140
  125.6 2.7 copy-done
  128.2 2.9 all-gather.2.cloned.1.call-done.u_ref
  131.2 3.1 %copy-done.4 = f32[4,4,128,896]{3,2,1,0:T(8,128)S(1)} copy-done((f32[4,4,128,896]{3,2,1,0:T(8,128)S(1)}, f32[4,4,128,896]{3,2,1,0:T(8,128)}, u32[]{:S(2)}) %copy-start.4) | copy-done | bytes 7340056
  134.2 73.9 %quantize_panels.1 = bf16[2048,4096]{1,0:T(8,128)(2,1)} custom-call(s32[32]{0:T(128)S(1)} %copy-done.5, bf16[2048,4096]{1,0:T(8,128)(2,1)} %w_ref.3, f32[4,4,128,896]{3,2,1,0:T(8,128)S(1)} %copy-done.4), custom_call_target="tpu_custom_call" | custom-call | flops 85899345920 | bytes 33554432 | tf_op jit(solution)/shard_map/quantize_panels/pallas_call | solution.py:235
  208.1 6.5 %copy-done.3 = bf16[2048,4096]{1,0:T(8,128)(2,1)S(1)} copy-done((bf16[2048,4096]{1,0:T(8,128)(2,1)S(1)}, bf16[2048,4096]{1,0:T(8,128)(2,1)}, u32[]{:S(2)}) %copy-start.3) | copy-done | bytes 16777240
  214.7 32.3 %error_products.3 = f32[8,4,128,128]{3,2,1,0:T(8,128)S(1)} custom-call(bf16[2048,4096]{1,0:T(8,128)(2,1)S(1)} %copy-done.3), custom_call_target="tpu_custom_call" | custom-call | flops 45634027520 | bytes 4194304 | tf_op jit(solution)/shard_map/error_products/pallas_call | solution.py:140
  247.0 1.2 slice.69
  248.2 2.7 slice_divide_fusion
  251.0 1.2 copy-done.6
  252.3 0.6 multiply_reduce_fusion
  253.8 39.4 %psum.15 = f32[128,4]{0,1:T(4,128)} all-reduce(f32[128,4]{0,1:T(4,128)S(1)} %dynamic_update_slice.3), channel_id=1, replica_groups=mesh['dp'=8,'tensor'=4] {'dp','tensor'}, use_global_device_ids=true, to_apply=%region_10.11 | all-reduce | flops 512 | bytes 4096 | tf_op jit(solution)/shard_map/psum | solution.py:309
  293.3 1.7 constant_dynamic-slice_fusion
  (32 shorter events, 1.5 us)
Async XLA Ops:
  7.2 124.0 %all-gather.2.cloned.1.call-start = ((), (), s32[]{:S(2)}) async-start(), calls=%async_computation | async-start | bytes 8257536 | tf_op jit(solution)/shard_map/all_gather | solution.py:283
  15.2 1.1 copy-start.7
  16.3 230.7 %all-reduce.2.cloned.1.call-start = ((), (), s32[]{:S(2)}) async-start(), calls=%async_computation.1 | async-start | bytes 4456448 | tf_op jit(solution)/shard_map/psum | solution.py:291
  16.5 2.2 copy-start.2
  125.5 2.7 copy-start
  128.2 2.9 copy-start.5
  131.2 3.1 %copy-start.4 = (f32[4,4,128,896]{3,2,1,0:T(8,128)S(1)}, f32[4,4,128,896]{3,2,1,0:T(8,128)}, u32[]{:S(2)}) copy-start(f32[4,4,128,896]{3,2,1,0:T(8,128)} %all-gather.2.cloned.1.call-done.u_ref) | copy-start | bytes 22020100
  208.1 6.5 %copy-start.3 = (bf16[2048,4096]{1,0:T(8,128)(2,1)S(1)}, bf16[2048,4096]{1,0:T(8,128)(2,1)}, u32[]{:S(2)}) copy-start(bf16[2048,4096]{1,0:T(8,128)(2,1)} %w_ref.3) | copy-start | bytes 50331652
  248.2 4.1 %copy-start.1 = (f32[24,4,128,128]{3,2,1,0:T(8,128)S(1)}, f32[24,4,128,128]{3,2,1,0:T(8,128)}, u32[]{:S(2)}) copy-start(f32[24,4,128,128]{3,2,1,0:T(8,128)} %copy-done) | copy-start | bytes 18874372
  250.9 1.4 copy-start.6
  252.3 1.0 slice-start
  252.9 0.8 copy-start.8
Sparse Core Ops, SparseCore 0:
  16.4 114.6 all-gather.1
  134.8 104.2 all-reduce.1
